TPU v7x, 32 devices: a whole 2x2x4 slice. The times are simulated.
32 devices in a mesh: groups: 2 (over x), tensor: 16 (over z, y, core).
Axes of the slice: x: 2, y: 2, z: 4, core: 2. Of those that a mesh axis runs over, the one named last changes fastest.
Arguments:
- queries: bfloat16 [64, 8192], P(('groups', 'tensor')), parts along dimension 0, may hold values from -5 to 5
- key_value_cache: bfloat16 [64, 512, 2, 1024], P(('groups', 'tensor')), parts along dimension 0, may hold values from -5 to 5
- live_cache_length: int32 [64], P(('groups', 'tensor')), parts along dimension 0, may hold values from 2 to 512
- residual: bfloat16 [64, 8192], P(('groups', 'tensor')), parts along dimension 0, may hold values from -2 to 2
- row_adapter_index: int32 [64, 1], P(('groups', 'tensor')), parts along dimension 0, may hold values from 0 to 15
- adapter_slot_index: int32 [16], replicated, may hold values from 0 to 15, each once
- output_projection_weight: bfloat16 [8192, 8192], P('tensor'), may hold values from -0.0625 to 0.0625
- adapter_down_weight: bfloat16 [16, 16, 8192], P('tensor'), may hold values from -0.0625 to 0.0625
- adapter_up_weight: bfloat16 [16, 16, 8192], P('tensor'), may hold values from -0.75 to 0.75
- norm_gain_weight: float32 [8192], replicated, may hold values from 0.5 to 1.5
Outputs:
- hidden: bfloat16 [64, 8192], P(('groups', 'tensor')), parts along dimension 0
- normed: bfloat16 [64, 8192], P(('groups', 'tensor')), parts along dimension 0
There are 2 independent parts, one for each index of `groups`. A program takes and returns all parts, laid end to end along the dimension named above; an argument that names none is the same for every part. Nothing has to cross between parts.
Inputs may be any that keep to these rules, and one draw needn't show every extreme that they name: `row_adapter_index`: every adapter is named by at least one row. `adapter_slot_index`: each slot holds exactly one adapter.
All inputs are finite; a program needn't handle non-finite values.
Results may differ from a plain program's by a relative error of at most 0.007.
Values may be sent and summed in bfloat16 or wider, within the bound.
A program may use at most 64 MiB of HBM per device.

v0:
```python
import math

import jax
import jax.numpy as jnp
from jax import lax
from jax.sharding import PartitionSpec as P

HQ = 64
KEY_HEADS = 8
HEAD_SIZE = 128
HEADS_PER_GROUP = 8


adapter_scale = 2.0
norm_eps = 1e-05
masked_score = -1e30


def attend(queries, key_value_cache, live_cache_length):
    count_of_rows = queries.shape[0]
    cache_capacity = key_value_cache.shape[1]
    heads_of_query = queries.reshape(count_of_rows, KEY_HEADS, HEADS_PER_GROUP, HEAD_SIZE)
    block_of_keys = key_value_cache[:, :, 0, :].reshape(
        count_of_rows, cache_capacity, KEY_HEADS, HEAD_SIZE
    )
    block_of_values = key_value_cache[:, :, 1, :].reshape(
        count_of_rows, cache_capacity, KEY_HEADS, HEAD_SIZE
    )
    scores = jnp.einsum(
        "rhgd,rchd->rhgc", heads_of_query, block_of_keys, preferred_element_type=jnp.float32
    )
    scores = scores * (1.0 / math.sqrt(HEAD_SIZE))
    live_mask = (jnp.arange(cache_capacity, dtype=jnp.int32)[None, :] < live_cache_length[:, None])[
        :, None, None, :
    ]
    scores = jnp.where(live_mask, scores, masked_score)
    top_score = jnp.max(scores, axis=-1, keepdims=True)
    weights_raw = jnp.where(live_mask, jnp.exp(scores - top_score), 0.0)
    weights_low = (weights_raw / jnp.sum(weights_raw, axis=-1, keepdims=True)).astype(jnp.bfloat16)
    mixed = jnp.einsum(
        "rhgc,rchd->rhgd", weights_low, block_of_values, preferred_element_type=jnp.float32
    )
    return mixed.astype(jnp.bfloat16).reshape(count_of_rows, HQ * HEAD_SIZE)


def rows_to_shrink(tile_of_rows, selector, adapter_down_weight):
    shrink_factor = jnp.einsum(
        "dz,gz->dg", tile_of_rows, adapter_down_weight[0], preferred_element_type=jnp.float32
    )
    return (shrink_factor * selector).astype(jnp.bfloat16)


def shards(
    queries,
    key_value_cache,
    live_cache_length,
    residual,
    row_adapter_index,
    adapter_slot_index,
    output_projection_weight,
    adapter_down_weight,
    adapter_up_weight,
    norm_gain_weight,
):
    device_count = lax.axis_size("tensor")
    my_index = lax.axis_index("tensor")
    mixed = attend(queries, key_value_cache, live_cache_length)
    slot_hot = (
        row_adapter_index == jnp.arange(adapter_slot_index.shape[0], dtype=jnp.int32)[None, :]
    )
    owner_index = jnp.sum(jnp.where(slot_hot, adapter_slot_index[None, :], 0), axis=1)
    owner_hot = owner_index[:, None] == jnp.arange(device_count, dtype=jnp.int32)[None, :]
    gathered_rows, mark_rows = (
        lax.all_gather(mixed, "tensor", axis=0, tiled=True),
        lax.all_gather(owner_hot.astype(jnp.bfloat16), "tensor", axis=0, tiled=True),
    )
    owned_row_marks = lax.dynamic_slice_in_dim(mark_rows, my_index, 1, 1).astype(jnp.float32)
    width = output_projection_weight.shape[0]
    features = lax.dynamic_slice_in_dim(gathered_rows, my_index * width, width, 1)
    base_tile = jnp.dot(features, output_projection_weight, preferred_element_type=jnp.float32)
    shrink_factor = rows_to_shrink(gathered_rows, owned_row_marks, adapter_down_weight)
    delta_tile = (
        adapter_scale
        * jnp.dot(shrink_factor, adapter_up_weight[0], preferred_element_type=jnp.float32)
    ).astype(jnp.bfloat16)
    projected = lax.psum_scatter(
        base_tile + delta_tile.astype(jnp.float32), "tensor", scatter_dimension=0, tiled=True
    )
    hidden_sum = residual.astype(jnp.float32) + projected
    mean_square = jnp.mean(hidden_sum * hidden_sum, axis=-1, keepdims=True)
    normed = hidden_sum * lax.rsqrt(mean_square + norm_eps) * norm_gain_weight
    return (hidden_sum.astype(jnp.bfloat16), normed.astype(jnp.bfloat16))


def solution(mesh):
    in_specs = (
        P(("groups", "tensor"), None),
        P(("groups", "tensor"), None, None, None),
        P(("groups", "tensor")),
        P(("groups", "tensor"), None),
        P(("groups", "tensor"), None),
        P(),
        P("tensor", None),
        P("tensor", None, None),
        P("tensor", None, None),
        P(),
    )
    out_specs = (P(("groups", "tensor"), None), P(("groups", "tensor"), None))
    return jax.shard_map(shards, mesh=mesh, in_specs=in_specs, out_specs=out_specs, check_vma=False)
```

profile of v0, /device:TPU:0, one launch (start us, length us, event | category | flops | bytes accessed | tf_op | source)
XLA Modules:
  0.0 190.7 jit_solution(2646145741992798659)
XLA Ops:
  7.2 0.0 copy-start
  7.2 0.0 all-reduce.3.cloned.1.call-start
  7.2 10.0 %fusion.20 = (bf16[2,512,1,1024]{3,2,1,0:T(2,128)(2,1)}, bf16[2,512,1,1024]{3,2,1,0:T(2,128)(2,1)}) fusion(bf16[2,512,2,1024]{3,2,1,0:T(2,128)(2,1)} %param.11), kind=kLoop, calls=%fused_computation.34 | loop fusion | bytes 8388608 | tf_op jit(solution)/shard_map/slice | solution.py:23
  17.3 0.0 copy-start.5
  17.3 9.0 %copy.31 = bf16[2,512,1,1024]{1,3,0,2:T(8,128)(2,1)S(1)} copy(bf16[2,512,1,1024]{3,2,1,0:T(2,128)(2,1)} %get-tuple-element.3) | data formatting | bytes 4194304
  26.3 0.0 copy-done.5
  26.3 0.0 copy-start.3
  26.3 0.1 iota_compare_fusion
  26.4 10.5 %copy.30 = bf16[2,512,1,1024]{1,3,0,2:T(8,128)(2,1)} copy(bf16[2,512,1,1024]{3,2,1,0:T(2,128)(2,1)} %get-tuple-element.2) | data formatting | bytes 4194304
  36.9 0.0 copy-start.6
  36.9 0.0 copy-start.7
  36.9 0.0 copy-start.1
  36.9 0.0 copy-done.3
  36.9 2.2 %fusion.21 = (f32[2,8,8]{2,1,0:T(8,128)S(1)}, f32[2,8,8,512]{3,2,1,0:T(8,128)S(1)}) fusion(pred[2,512]{1,0:T(4,128)(4,1)S(1)} %iota_compare_fusion, bf16[2,512,8,128]{1,3,2,0:T(8,128)(2,1)} %bitcast.31, bf16[1,2,64,128]{3,1,2,0:T(2,128)(2,1)S(1)} %bitcast.32), kind=kOutput, calls=%fused_computation.35 | convolution fusion | flops 17105408 | bytes 2393600 | tf_op jit(solution)/shard_map/sub | solution.py:38
  39.1 0.7 convolution_convert_fusion
  39.8 24.6 %all-gather = bf16[16,2,8192]{2,1,0:T(2,128)(2,1)S(1)} all-gather(bf16[1,2,8192]{2,1,0:T(2,128)(2,1)S(1)} %reshape.43), channel_id=1, replica_groups=mesh['groups'=2,'tensor'=16] {'tensor'}, dimensions={0}, use_global_device_ids=true | all-gather | bytes 557056 | tf_op jit(solution)/shard_map/all_gather | solution.py:74
  64.4 0.2 reshape.44
  64.6 0.0 copy-done.6
  64.6 0.0 copy-done.7
  64.6 0.2 fusion.16
  64.8 0.1 fusion.17
  64.9 17.3 %all-gather.1 = bf16[16,2,16]{2,1,0:T(2,128)(2,1)S(1)} all-gather(bf16[1,2,16]{2,1,0:T(2,128)(2,1)S(1)} %fusion.17), channel_id=1, replica_groups=mesh['groups'=2,'tensor'=16] {'tensor'}, dimensions={0}, use_global_device_ids=true | all-gather | bytes 1088 | tf_op jit(solution)/shard_map/all_gather | solution.py:75
  82.2 0.1 constant_dynamic-slice_fusion
  82.3 0.1 copy.32
  82.4 0.0 copy-done
  82.4 0.0 copy-done.1
  82.4 0.8 fusion.2
  83.2 0.0 copy-start.8
  83.2 0.0 copy-start.2
  83.2 0.0 copy-start.4
  83.3 6.0 %convolution_add_fusion = f32[32,8192]{1,0:T(8,128)} fusion(f32[32,8192]{1,0:T(8,128)S(1)} %fusion.2, bf16[512,8192]{1,0:T(8,128)(2,1)} %param.16, bf16[32,8192]{1,0:T(8,128)(2,1)S(1)} %reshape.44, s32[]{:T(128)S(6)} %select_n.19), kind=kOutput, calls=%fused_computation.2 | convolution fusion | flops 268697600 | bytes 10518532 | tf_op jit(solution)/shard_map/dot_general | solution.py:80
  89.2 0.0 all-reduce.3.cloned.1.call-update
  89.3 0.0 copy-done.8
  89.3 0.6 dynamic-slice
  90.5 90.5 %all-reduce.3.cloned.1.call-done = f32[32,8192]{1,0:T(8,128)} async-done(((f32[32,8192]{1,0:T(8,128)}), f32[32,8192]{1,0:T(8,128)}) %all-reduce.3.cloned.1.call-update) | async-done | bytes 1048592
  181.0 0.0 copy-done.2
  181.0 1.1 multiply_reduce_fusion
  182.1 0.0 copy-done.4
  182.1 1.7 multiply_convert_fusion
  (3 shorter events, 0.0 us)
Async XLA Ops:
  7.2 75.2 %copy-start = (bf16[1,16,8192]{2,1,0:T(8,128)(2,1)S(1)}, bf16[1,16,8192]{2,1,0:T(8,128)(2,1)}, u32[]{:S(2)}) copy-start(bf16[1,16,8192]{2,1,0:T(8,128)(2,1)} %param.18) | copy-start | bytes 786436
  7.2 173.8 %all-reduce.3.cloned.1.call-start = ((), (), s32[]{:S(2)}) async-start(), calls=%async_computation | async-start | bytes 2097152
  17.3 9.0 %copy-start.5 = (s32[2]{0:T(128)S(1)}, s32[2]{0:T(128)}, u32[]{:S(2)}) copy-start(s32[2]{0:T(128)} %param.12) | copy-start | bytes 28
  26.3 10.6 %copy-start.3 = (bf16[2,8192]{1,0:T(2,128)(2,1)S(1)}, bf16[2,8192]{1,0:T(2,128)(2,1)}, u32[]{:S(2)}) copy-start(bf16[2,8192]{1,0:T(2,128)(2,1)} %param.10) | copy-start | bytes 98308
  36.9 27.7 %copy-start.6 = (s32[16]{0:T(128)S(1)}, s32[16]{0:T(128)}, u32[]{:S(2)}) copy-start(s32[16]{0:T(128)} %param.15) | copy-start | bytes 196
  36.9 27.7 %copy-start.7 = (s32[2,1]{0,1:T(1,128)S(1)}, s32[2,1]{0,1:T(1,128)}, u32[]{:S(2)}) copy-start(s32[2,1]{0,1:T(1,128)} %param.14) | copy-start | bytes 28
  36.9 45.5 %copy-start.1 = (bf16[1,16,8192]{2,1,0:T(8,128)(2,1)S(1)}, bf16[1,16,8192]{2,1,0:T(8,128)(2,1)}, u32[]{:S(2)}) copy-start(bf16[1,16,8192]{2,1,0:T(8,128)(2,1)} %param.17) | copy-start | bytes 786436
  83.2 6.0 %copy-start.8 = (u32[32]{0:T(128)S(1)}, u32[32]{0:T(128)}, u32[]{:S(2)}) copy-start(u32[32]{0:T(128)} %constant.36) | copy-start | bytes 388
  83.2 97.8 %copy-start.2 = (bf16[2,8192]{1,0:T(2,128)(2,1)S(1)}, bf16[2,8192]{1,0:T(2,128)(2,1)}, u32[]{:S(2)}) copy-start(bf16[2,8192]{1,0:T(2,128)(2,1)} %param.13) | copy-start | bytes 98308
  83.2 98.9 %copy-start.4 = (f32[8192]{0:T(1024)S(1)}, f32[8192]{0:T(1024)}, u32[]{:S(2)}) copy-start(f32[8192]{0:T(1024)} %param.19) | copy-start | bytes 98308
Sparse Core Ops, SparseCore 0:
  89.4 91.5 all-reduce.2
where the time goes:
time: 191 us
  waiting for transfers between devices  90.5 us (47%)
  blocking collectives  41.9 us (22%)
  local copies, waits for them, and re-layouts  30.6 us (16%)
  between operations  14.8 us (8%)
  matrix products  9.68 us (5%)
  other arithmetic  3.15 us (2%)
    unnamed x2, waiting for transfers between devices  90.5 us
    all_gather x1, blocking collectives, shards(): lax.all_gather(mixed, 'tensor', axis=0, tiled=True)  24.6 us
    unnamed x24, local copies, waits for them, and re-layouts  20.5 us
    all_gather x1, blocking collectives, shards(): lax.all_gather(owner_hot.astype(jnp.bfloat16), 'tensor', axis=0, tiled=True)  17.3 us
    slice x1, local copies, waits for them, and re-layouts, attend(): key_value_cache[:, :, 0, :]  10 us
    dot_general x1, matrix products, shards(): jnp.dot(features, output_projection_weight, preferred_element_type=jnp.fl...  5.97 us
  transfers between devices with their start and end apart: 1, of which 1 were waited for; matrix products, arithmetic and copies ran while one was open for 0% of the time, Pallas kernels for 0%

commit v1 on v0

--- a/solution.py
+++ b/solution.py
@@ -1,8 +1,11 @@
+import functools
 import math
 
 import jax
 import jax.numpy as jnp
 from jax import lax
+from jax.experimental import pallas as pl
+from jax.experimental.pallas import tpu as pltpu
 from jax.sharding import PartitionSpec as P
 
 HQ = 64
@@ -92,6 +95,375 @@
     return (hidden_sum.astype(jnp.bfloat16), normed.astype(jnp.bfloat16))
 
 
+CHUNKS = 4
+LANES = 128
+
+
+def remote(source, target, send_sem, recv_sem, peer):
+    return pltpu.make_async_remote_copy(
+        src_ref=source,
+        dst_ref=target,
+        send_sem=send_sem,
+        recv_sem=recv_sem,
+        device_id={"tensor": peer},
+        device_id_type=pl.DeviceIdType.MESH,
+    )
+
+
+def fused(
+    count,
+    depth,
+    q_ref,
+    cache_ref,
+    live_ref,
+    residual_ref,
+    row_adapter_ref,
+    slot_ref,
+    weight_ref,
+    down_ref,
+    up_ref,
+    gain_ref,
+    hidden_ref,
+    normed_ref,
+    cache,
+    weight,
+    message,
+    arrived,
+    features,
+    down,
+    shrink_out,
+    shrink_in,
+    part,
+    core_in,
+    y_out,
+    y_in,
+    z_out,
+    z_in,
+    total,
+    cache_sem,
+    weight_sem,
+    message_send,
+    message_recv,
+    down_send,
+    down_recv,
+    down_local,
+    shrink_send,
+    shrink_recv,
+    core_send,
+    core_recv,
+    y_send,
+    y_recv,
+    z_send,
+    z_recv,
+):
+    me = lax.axis_index("tensor")
+    my_core = me % 2
+    my_y = (me // 2) % 2
+    my_z = me // 4
+    core_peer = me + 1 - 2 * my_core
+    y_peer = me + 2 - 4 * my_y
+    row_count = 2 * count
+    columns = weight_ref.shape[1] // CHUNKS
+
+    cache_copies = [
+        pltpu.make_async_copy(cache_ref.at[b], cache.at[b], cache_sem.at[b]) for b in range(2)
+    ]
+    weight_copies = [
+        pltpu.make_async_copy(
+            weight_ref.at[:, pl.ds(j * columns, columns)], weight.at[j], weight_sem.at[j]
+        )
+        for j in range(CHUNKS)
+    ]
+    for copy in cache_copies + weight_copies:
+        copy.start()
+
+    barrier = pltpu.get_barrier_semaphore()
+
+    @pl.loop(1, count)
+    def _(step):
+        pl.semaphore_signal(
+            barrier,
+            inc=1,
+            device_id={"tensor": (me + step) % count},
+            device_id_type=pl.DeviceIdType.MESH,
+        )
+
+    pl.semaphore_wait(barrier, count - 1)
+
+    def down_copy(peer, source):
+        return remote(
+            down_ref.at[0, :, pl.ds(pl.multiple_of(peer * depth, depth), depth)],
+            down.at[source],
+            down_send.at[peer],
+            down_recv.at[source],
+            peer,
+        )
+
+    @pl.loop(1, count)
+    def _(step):
+        down_copy((me + step) % count, me).start()
+
+    own_down = pltpu.make_async_copy(
+        down_ref.at[0, :, pl.ds(pl.multiple_of(me * depth, depth), depth)],
+        down.at[me],
+        down_local.at[0],
+    )
+    own_down.start()
+
+    adapters = slot_ref.shape[1]
+    named = lax.broadcasted_iota(jnp.int32, (2, adapters), 1) == row_adapter_ref[...]
+    owner = jnp.sum(
+        jnp.where(named, slot_ref[...].astype(jnp.float32), 0.0), axis=1, keepdims=True
+    )
+    owner_block = jnp.broadcast_to(owner, (2, LANES)).astype(jnp.bfloat16)
+
+    def message_copy(peer, source):
+        return remote(
+            message.at[peer], arrived.at[source], message_send.at[peer], message_recv.at[source], peer
+        )
+
+    for copy in cache_copies:
+        copy.wait()
+    positions = cache_ref.shape[1] * 2
+    lane = lax.broadcasted_iota(jnp.int32, (HEADS_PER_GROUP, positions), 1)
+
+    @pl.loop(0, KEY_HEADS)
+    def _(head):
+        heads = q_ref[
+            :, pl.ds(pl.multiple_of(head * HEADS_PER_GROUP * HEAD_SIZE, 1024), HEADS_PER_GROUP * HEAD_SIZE)
+        ].astype(jnp.float32)
+        found = []
+        for b in range(2):
+            query = jnp.concatenate(
+                [
+                    heads[b : b + 1, g * HEAD_SIZE : (g + 1) * HEAD_SIZE]
+                    for g in range(HEADS_PER_GROUP)
+                ],
+                axis=0,
+            ).astype(jnp.bfloat16)
+            pairs = cache[b, :, :, pl.ds(pl.multiple_of(head * HEAD_SIZE, HEAD_SIZE), HEAD_SIZE)].reshape(
+                positions, HEAD_SIZE
+            )
+            scores = lax.dot_general(
+                query, pairs, (((1,), (1,)), ((), ())), preferred_element_type=jnp.float32
+            ) * (1.0 / math.sqrt(HEAD_SIZE))
+            live = jnp.logical_and(lane < 2 * live_ref[b], lane % 2 == 0)
+            scores = jnp.where(live, scores, masked_score)
+            top = jnp.max(scores, axis=-1, keepdims=True)
+            raw = jnp.where(live, jnp.exp(scores - top), 0.0)
+            weights = raw / jnp.sum(raw, axis=-1, keepdims=True)
+            weights = pltpu.roll(weights, 1, 1).astype(jnp.bfloat16)
+            found.append(jnp.dot(weights, pairs, preferred_element_type=jnp.float32))
+        for half in range(2):
+            rows = [
+                jnp.concatenate([f[half * 4 + g : half * 4 + g + 1] for g in range(4)], axis=1)
+                for f in found
+            ]
+            peer = 2 * head + half
+            message[peer, :, :depth] = jnp.concatenate(rows, axis=0).astype(jnp.bfloat16)
+            message[peer, :, depth:] = owner_block
+
+            @pl.when(peer != me)
+            def _():
+                message_copy(peer, me).start()
+
+    arrived[me] = message[me]
+
+    @pl.loop(1, count)
+    def _(step):
+        message_copy((me + step) % count, (me + step) % count).wait_recv()
+
+    for source in range(count):
+        z, y, c = source // 4, (source // 2) % 2, source % 2
+        place = ((c * 2 + y) * 4 + z) * 2
+        features[place : place + 2, :] = arrived[source].astype(jnp.float32)
+    owners = features[:, depth : depth + 1]
+    mine = features[:, :depth].astype(jnp.bfloat16)
+
+    own_down.wait()
+
+    @pl.loop(1, count)
+    def _(step):
+        down_copy((me + step) % count, (me + step) % count).wait_recv()
+
+    rank = down_ref.shape[1]
+    shrink_out[...] = lax.dot_general(
+        down[...].reshape(count * rank, depth),
+        mine,
+        (((1,), (1,)), ((), ())),
+        preferred_element_type=jnp.float32,
+    ).reshape(count, rank, row_count)
+
+    def shrink_copy(peer, source):
+        return remote(
+            shrink_out.at[peer], shrink_in.at[source], shrink_send.at[peer], shrink_recv.at[source], peer
+        )
+
+    @pl.loop(1, count)
+    def _(step):
+        shrink_copy((me + step) % count, me).start()
+
+    shrink_in[me] = shrink_out[me]
+
+    for j in range(CHUNKS):
+        weight_copies[j].wait()
+        part[j] = jnp.dot(mine, weight[j], preferred_element_type=jnp.float32).reshape(
+            2, count, columns
+        )
+
+    @pl.loop(1, count)
+    def _(step):
+        shrink_copy((me + step) % count, (me + step) % count).wait_recv()
+
+    shrink = jnp.sum(shrink_in[...], axis=0).astype(jnp.bfloat16)
+    owned = owners == me.astype(jnp.float32)
+
+    core_copies = [
+        remote(part.at[j, 1 - my_core], core_in.at[j], core_send.at[j], core_recv.at[j], core_peer)
+        for j in range(CHUNKS)
+    ]
+    y_copies = [
+        remote(y_out.at[j, 1 - my_y], y_in.at[j], y_send.at[j], y_recv.at[j], y_peer)
+        for j in range(CHUNKS)
+    ]
+
+    def z_copy(j, step):
+        return remote(
+            z_out.at[j, (my_z + step) % 4],
+            z_in.at[j, step],
+            z_send.at[j, step],
+            z_recv.at[j, step],
+            (me + 4 * step) % count,
+        )
+
+    for j in range(CHUNKS):
+        delta = (
+            adapter_scale
+            * lax.dot_general(
+                shrink,
+                up_ref[0, :, j * columns : (j + 1) * columns],
+                (((0,), (0,)), ((), ())),
+                preferred_element_type=jnp.float32,
+            )
+        ).astype(jnp.bfloat16)
+        delta = jnp.where(owned, delta.astype(jnp.float32), 0.0)
+        part[j] = part[j] + delta.reshape(2, count, columns)
+        core_copies[j].start()
+    for j in range(CHUNKS):
+        core_copies[j].wait_recv()
+        chip_sum = part[j, my_core] + core_in[j]
+        y_out[j] = chip_sum.reshape(2, count // 2, columns).astype(jnp.bfloat16)
+        y_copies[j].start()
+    for j in range(CHUNKS):
+        y_copies[j].wait_recv()
+        pair_sum = y_out[j, my_y].astype(jnp.float32) + y_in[j].astype(jnp.float32)
+        for z in range(4):
+            z_out[j, z] = pair_sum[2 * z : 2 * z + 2].astype(jnp.bfloat16)
+        for step in range(1, 4):
+            z_copy(j, step).start()
+    square = jnp.zeros((2, 1), jnp.float32)
+    for j in range(CHUNKS):
+        here = slice(j * columns, (j + 1) * columns)
+        value = residual_ref[:, here].astype(jnp.float32) + z_out[j, my_z].astype(jnp.float32)
+        for step in range(1, 4):
+            z_copy(j, step).wait_recv()
+            value = value + z_in[j, step].astype(jnp.float32)
+        total[:, here] = value
+        hidden_ref[:, here] = value.astype(jnp.bfloat16)
+        square = square + jnp.sum(value * value, axis=1, keepdims=True)
+    scale = lax.rsqrt(square / weight_ref.shape[1] + norm_eps)
+    normed_ref[...] = (total[...] * scale * gain_ref[...]).astype(jnp.bfloat16)
+
+    @pl.loop(1, count)
+    def _(step):
+        peer = (me + step) % count
+        message_copy(peer, me).wait_send()
+        down_copy(peer, me).wait_send()
+        shrink_copy(peer, me).wait_send()
+
+    for j in range(CHUNKS):
+        core_copies[j].wait_send()
+        y_copies[j].wait_send()
+        for step in range(1, 4):
+            z_copy(j, step).wait_send()
+
+
+def fused_call(
+    queries,
+    key_value_cache,
+    live_cache_length,
+    residual,
+    row_adapter_index,
+    adapter_slot_index,
+    output_projection_weight,
+    adapter_down_weight,
+    adapter_up_weight,
+    norm_gain_weight,
+):
+    count = lax.axis_size("tensor")
+    depth, width = output_projection_weight.shape
+    columns = width // CHUNKS
+    rank = adapter_down_weight.shape[1]
+    vmem = pl.BlockSpec(memory_space=pltpu.VMEM)
+    hbm = pl.BlockSpec(memory_space=pl.ANY)
+    smem = pl.BlockSpec(memory_space=pltpu.SMEM)
+    dma = pltpu.SemaphoreType.DMA
+    f32, bf16 = jnp.float32, jnp.bfloat16
+    row = jax.ShapeDtypeStruct((2, width), bf16)
+    return pl.pallas_call(
+        functools.partial(fused, count, depth),
+        out_shape=(row, row),
+        in_specs=[vmem, hbm, smem, vmem, vmem, vmem, hbm, hbm, vmem, vmem],
+        out_specs=(vmem, vmem),
+        scratch_shapes=[
+            pltpu.VMEM(key_value_cache.shape, bf16),
+            pltpu.VMEM((CHUNKS, depth, columns), bf16),
+            pltpu.VMEM((count, 2, depth + LANES), bf16),
+            pltpu.VMEM((count, 2, depth + LANES), bf16),
+            pltpu.VMEM((2 * count, depth + LANES), f32),
+            pltpu.VMEM((count, rank, depth), bf16),
+            pltpu.VMEM((count, rank, 2 * count), f32),
+            pltpu.VMEM((count, rank, 2 * count), f32),
+            pltpu.VMEM((CHUNKS, 2, count, columns), f32),
+            pltpu.VMEM((CHUNKS, count, columns), f32),
+            pltpu.VMEM((CHUNKS, 2, count // 2, columns), bf16),
+            pltpu.VMEM((CHUNKS, count // 2, columns), bf16),
+            pltpu.VMEM((CHUNKS, 4, 2, columns), bf16),
+            pltpu.VMEM((CHUNKS, 4, 2, columns), bf16),
+            pltpu.VMEM((2, width), f32),
+            dma((2,)),
+            dma((CHUNKS,)),
+            dma((count,)),
+            dma((count,)),
+            dma((count,)),
+            dma((count,)),
+            dma((1,)),
+            dma((count,)),
+            dma((count,)),
+            dma((CHUNKS,)),
+            dma((CHUNKS,)),
+            dma((CHUNKS,)),
+            dma((CHUNKS,)),
+            dma((CHUNKS, 4)),
+            dma((CHUNKS, 4)),
+        ],
+        compiler_params=pltpu.CompilerParams(
+            collective_id=0, has_side_effects=True, vmem_limit_bytes=48 * 1024 * 1024
+        ),
+    )(
+        queries,
+        key_value_cache,
+        live_cache_length,
+        residual,
+        row_adapter_index,
+        adapter_slot_index.reshape(1, -1),
+        output_projection_weight,
+        adapter_down_weight,
+        adapter_up_weight,
+        norm_gain_weight.reshape(1, -1),
+    )
+
+
 def solution(mesh):
     in_specs = (
         P(("groups", "tensor"), None),
@@ -106,4 +478,5 @@
         P(),
     )
     out_specs = (P(("groups", "tensor"), None), P(("groups", "tensor"), None))
-    return jax.shard_map(shards, mesh=mesh, in_specs=in_specs, out_specs=out_specs, check_vma=False)
+    body = fused_call if mesh.shape["tensor"] == 16 else shards
+    return jax.shard_map(body, mesh=mesh, in_specs=in_specs, out_specs=out_specs, check_vma=False)

time: 191 us -> 45.8 us (0.24)
  waiting for transfers between devices: 90.5 us -> 0 us
  blocking collectives: 41.9 us -> 0 us
  Pallas kernels: 0 us -> 35.1 us
  local copies, waits for them, and re-layouts: 30.6 us -> 9.64 us
  between operations: 14.8 us -> 0.65 us
  matrix products: 9.68 us -> 0 us
  other arithmetic: 3.15 us -> 0 us
    unnamed x2 -> x0, waiting for transfers between devices: 90.5 us -> none
    all_gather x2 -> x0, blocking collectives: 41.9 us -> none  [the longest x1 24.6 us: shards(): lax.all_gather(mixed, 'tensor', axis=0, tiled=True)]
    pallas_call x0 -> x1, Pallas kernels: none -> 35.1 us  [fused_call(): pl.pallas_call(functools.partial(fused, count, depth), out_shape=(row, ro...]
    unnamed x24 -> x19, local copies, waits for them, and re-layouts: 20.5 us -> 9.64 us
    slice x1 -> x0, local copies, waits for them, and re-layouts: 10 us -> none  [attend(): key_value_cache[:, :, 0, :]]
    dot_general x3 -> x0, matrix products: 7.49 us -> none  [the longest x1 5.97 us: shards(): jnp.dot(features, output_projection_weight, preferred_element_type=jnp.fl...]
    sub x1 -> x0, matrix products: 2.19 us -> none  [attend(): weights_raw = jnp.where(live_mask, jnp.exp(scores - top_score), 0.0)]
  transfers between devices with their start and end apart: 1 -> 0, of which waited for: 1 -> 0; matrix products, arithmetic and copies ran while one was open for 0% -> 0% of each run, Pallas kernels for 0% -> 0%
where the time goes in v1:
time: 45.8 us; the launch traced here: 45.4 us
  Pallas kernels  35.1 us (77%)
  local copies, waits for them, and re-layouts  9.64 us (21%)
  between operations  0.65 us (1%)
    pallas_call x1, Pallas kernels, fused_call(): pl.pallas_call(functools.partial(fused, count, depth), out_shape=(row, ro...  35.1 us
    unnamed x19, local copies, waits for them, and re-layouts  9.64 us

profile of v1, /device:TPU:0, one launch (start us, length us, event | category | flops | bytes accessed | tf_op | source)
XLA Modules:
  0.0 45.4 jit_solution(11377075989477238106)
XLA Ops:
  0.6 0.7 %copy.12.row_adapter_ref = s32[2,1]{1,0:T(2,128)S(1)} copy(s32[2,1]{0,1:T(1,128)} %param.14) | data formatting | bytes 16 | tf_op args[4]
  1.4 0.0 copy-start
  1.4 2.2 %copy-done = bf16[2,512,2,1024]{3,2,1,0:T(2,128)(2,1)S(1)} copy-done((bf16[2,512,2,1024]{3,2,1,0:T(2,128)(2,1)S(1)}, bf16[2,512,2,1024]{3,2,1,0:T(2,128)(2,1)}, u32[]{:S(2)}) %copy-start) | copy-done | bytes 4194328
  3.6 0.0 copy-start.1
  3.6 0.9 %copy-done.1 = bf16[1,16,8192]{2,1,0:T(8,128)(2,1)S(1)} copy-done((bf16[1,16,8192]{2,1,0:T(8,128)(2,1)S(1)}, bf16[1,16,8192]{2,1,0:T(8,128)(2,1)}, u32[]{:S(2)}) %copy-start.1) | copy-done | bytes 262168
  4.5 0.0 copy-start.2
  4.5 0.9 %copy-done.2 = bf16[1,16,8192]{2,1,0:T(8,128)(2,1)S(1)} copy-done((bf16[1,16,8192]{2,1,0:T(8,128)(2,1)S(1)}, bf16[1,16,8192]{2,1,0:T(8,128)(2,1)}, u32[]{:S(2)}) %copy-start.2) | copy-done | bytes 262168
  5.5 0.0 copy-start.3
  5.5 0.8 %copy-done.3 = bf16[2,8192]{1,0:T(2,128)(2,1)S(1)} copy-done((bf16[2,8192]{1,0:T(2,128)(2,1)S(1)}, bf16[2,8192]{1,0:T(2,128)(2,1)}, u32[]{:S(2)}) %copy-start.3) | copy-done | bytes 32792
  6.2 0.0 copy-start.4
  6.2 0.8 %copy-done.4 = bf16[2,8192]{1,0:T(2,128)(2,1)S(1)} copy-done((bf16[2,8192]{1,0:T(2,128)(2,1)S(1)}, bf16[2,8192]{1,0:T(2,128)(2,1)}, u32[]{:S(2)}) %copy-start.4) | copy-done | bytes 32792
  7.0 0.0 copy-start.5
  7.0 0.8 %copy-done.5 = f32[8192]{0:T(1024)S(1)} copy-done((f32[8192]{0:T(1024)S(1)}, f32[8192]{0:T(1024)}, u32[]{:S(2)}) %copy-start.5) | copy-done | bytes 32792
  7.7 0.0 copy-start.6
  7.7 0.7 %copy-done.6 = s32[2]{0:T(128)S(1)} copy-done((s32[2]{0:T(128)S(1)}, s32[2]{0:T(128)}, u32[]{:S(2)}) %copy-start.6) | copy-done | bytes 32
  8.4 0.0 copy-start.7
  8.4 0.7 %copy-done.7 = s32[16]{0:T(128)S(1)} copy-done((s32[16]{0:T(128)S(1)}, s32[16]{0:T(128)}, u32[]{:S(2)}) %copy-start.7) | copy-done | bytes 88
  9.0 35.1 %shard_map.113 = (bf16[2,8192]{1,0:T(2,128)(2,1)S(1)}, bf16[2,8192]{1,0:T(2,128)(2,1)S(1)}) custom-call(bf16[2,8192]{1,0:T(2,128)(2,1)S(1)} %copy-done.3, bf16[2,512,2,1024]{3,2,1,0:T(2,128)(2,1)S(1)} %copy-done, s32[2]{0:T(128)S(1)} %copy-done.6, bf16[2,8192]{1,0:T(2,128)(2,1)S(1)} %copy-done.4, s32[2,1]{1,0:T(2,128)S(1)} %copy.12.row_adapter_ref, ...), custom_call_target="tpu_custom_call" | custom-call | tf_op jit(solution)/shard_map/pallas_call | solution.py:413
  44.2 0.6 %copy.15 = bf16[2,8192]{1,0:T(2,128)(2,1)} copy(bf16[2,8192]{1,0:T(2,128)(2,1)S(1)} %get-tuple-element.4) | data formatting | bytes 65536
  44.8 0.6 %copy.16 = bf16[2,8192]{1,0:T(2,128)(2,1)} copy(bf16[2,8192]{1,0:T(2,128)(2,1)S(1)} %get-tuple-element.5) | data formatting | bytes 65536
Async XLA Ops:
  1.4 2.2 %copy-start = (bf16[2,512,2,1024]{3,2,1,0:T(2,128)(2,1)S(1)}, bf16[2,512,2,1024]{3,2,1,0:T(2,128)(2,1)}, u32[]{:S(2)}) copy-start(bf16[2,512,2,1024]{3,2,1,0:T(2,128)(2,1)} %cache_ref.1) | copy-start | bytes 12582916
  3.6 0.9 %copy-start.1 = (bf16[1,16,8192]{2,1,0:T(8,128)(2,1)S(1)}, bf16[1,16,8192]{2,1,0:T(8,128)(2,1)}, u32[]{:S(2)}) copy-start(bf16[1,16,8192]{2,1,0:T(8,128)(2,1)} %down_ref.1) | copy-start | bytes 786436
  4.5 0.9 %copy-start.2 = (bf16[1,16,8192]{2,1,0:T(8,128)(2,1)S(1)}, bf16[1,16,8192]{2,1,0:T(8,128)(2,1)}, u32[]{:S(2)}) copy-start(bf16[1,16,8192]{2,1,0:T(8,128)(2,1)} %up_ref.1) | copy-start | bytes 786436
  5.5 0.8 %copy-start.3 = (bf16[2,8192]{1,0:T(2,128)(2,1)S(1)}, bf16[2,8192]{1,0:T(2,128)(2,1)}, u32[]{:S(2)}) copy-start(bf16[2,8192]{1,0:T(2,128)(2,1)} %q_ref.1) | copy-start | bytes 98308
  6.2 0.8 %copy-start.4 = (bf16[2,8192]{1,0:T(2,128)(2,1)S(1)}, bf16[2,8192]{1,0:T(2,128)(2,1)}, u32[]{:S(2)}) copy-start(bf16[2,8192]{1,0:T(2,128)(2,1)} %residual_ref.1) | copy-start | bytes 98308
  7.0 0.8 %copy-start.5 = (f32[8192]{0:T(1024)S(1)}, f32[8192]{0:T(1024)}, u32[]{:S(2)}) copy-start(f32[8192]{0:T(1024)} %param.19) | copy-start | bytes 98308
  7.7 0.7 %copy-start.6 = (s32[2]{0:T(128)S(1)}, s32[2]{0:T(128)}, u32[]{:S(2)}) copy-start(s32[2]{0:T(128)} %live_ref.1) | copy-start | bytes 28
  8.4 0.7 %copy-start.7 = (s32[16]{0:T(128)S(1)}, s32[16]{0:T(128)}, u32[]{:S(2)}) copy-start(s32[16]{0:T(128)} %param.15) | copy-start | bytes 196

commit v2 on v1

--- a/solution.py
+++ b/solution.py
@@ -113,18 +113,26 @@
 def fused(
     count,
     depth,
+    q_hbm,
+    cache_ref,
+    live_hbm,
+    residual_hbm,
+    row_adapter_hbm,
+    slot_hbm,
+    weight_ref,
+    down_ref,
+    up_hbm,
+    gain_hbm,
+    hidden_ref,
+    normed_ref,
     q_ref,
-    cache_ref,
     live_ref,
     residual_ref,
     row_adapter_ref,
     slot_ref,
-    weight_ref,
-    down_ref,
     up_ref,
     gain_ref,
-    hidden_ref,
-    normed_ref,
+    small_sem,
     cache,
     weight,
     message,
@@ -174,7 +182,13 @@
         )
         for j in range(CHUNKS)
     ]
-    for copy in cache_copies + weight_copies:
+    early = [(q_hbm, q_ref), (live_hbm, live_ref), (row_adapter_hbm, row_adapter_ref), (slot_hbm, slot_ref)]
+    late = [(up_hbm, up_ref), (residual_hbm, residual_ref), (gain_hbm, gain_ref)]
+    small_copies = [
+        pltpu.make_async_copy(source, target, small_sem.at[i])
+        for i, (source, target) in enumerate(early + late)
+    ]
+    for copy in small_copies[: len(early)] + cache_copies + weight_copies + small_copies[len(early) :]:
         copy.start()
 
     barrier = pltpu.get_barrier_semaphore()
@@ -210,8 +224,13 @@
     )
     own_down.start()
 
+    for copy in small_copies[: len(early)]:
+        copy.wait()
     adapters = slot_ref.shape[1]
-    named = lax.broadcasted_iota(jnp.int32, (2, adapters), 1) == row_adapter_ref[...]
+    row_adapter = jnp.where(
+        lax.broadcasted_iota(jnp.int32, (2, adapters), 0) == 0, row_adapter_ref[0], row_adapter_ref[1]
+    )
+    named = lax.broadcasted_iota(jnp.int32, (2, adapters), 1) == row_adapter
     owner = jnp.sum(
         jnp.where(named, slot_ref[...].astype(jnp.float32), 0.0), axis=1, keepdims=True
     )
@@ -315,6 +334,8 @@
     def _(step):
         shrink_copy((me + step) % count, (me + step) % count).wait_recv()
 
+    for copy in small_copies[len(early) :]:
+        copy.wait()
     shrink = jnp.sum(shrink_in[...], axis=0).astype(jnp.bfloat16)
     owned = owners == me.astype(jnp.float32)
 
@@ -406,16 +427,23 @@
     rank = adapter_down_weight.shape[1]
     vmem = pl.BlockSpec(memory_space=pltpu.VMEM)
     hbm = pl.BlockSpec(memory_space=pl.ANY)
-    smem = pl.BlockSpec(memory_space=pltpu.SMEM)
     dma = pltpu.SemaphoreType.DMA
     f32, bf16 = jnp.float32, jnp.bfloat16
     row = jax.ShapeDtypeStruct((2, width), bf16)
     return pl.pallas_call(
         functools.partial(fused, count, depth),
         out_shape=(row, row),
-        in_specs=[vmem, hbm, smem, vmem, vmem, vmem, hbm, hbm, vmem, vmem],
+        in_specs=[hbm] * 10,
         out_specs=(vmem, vmem),
         scratch_shapes=[
+            pltpu.VMEM(queries.shape, bf16),
+            pltpu.SMEM(live_cache_length.shape, jnp.int32),
+            pltpu.VMEM(residual.shape, bf16),
+            pltpu.SMEM(live_cache_length.shape, jnp.int32),
+            pltpu.VMEM((1, adapter_slot_index.shape[0]), jnp.int32),
+            pltpu.VMEM(adapter_up_weight.shape, bf16),
+            pltpu.VMEM((1, width), f32),
+            dma((7,)),
             pltpu.VMEM(key_value_cache.shape, bf16),
             pltpu.VMEM((CHUNKS, depth, columns), bf16),
             pltpu.VMEM((count, 2, depth + LANES), bf16),
@@ -448,14 +476,14 @@
             dma((CHUNKS, 4)),
         ],
         compiler_params=pltpu.CompilerParams(
-            collective_id=0, has_side_effects=True, vmem_limit_bytes=48 * 1024 * 1024
+            collective_id=0, has_side_effects=True, vmem_limit_bytes=60 * 1024 * 1024
         ),
     )(
         queries,
         key_value_cache,
         live_cache_length,
         residual,
-        row_adapter_index,
+        row_adapter_index.reshape(-1),
         adapter_slot_index.reshape(1, -1),
         output_projection_weight,
         adapter_down_weight,

time: 45.8 us -> 38.7 us (0.84)
  local copies, waits for them, and re-layouts: 9.64 us -> 2.79 us
    unnamed x19 -> x2, local copies, waits for them, and re-layouts: 9.64 us -> 2.79 us
where the time goes in v2:
time: 38.7 us; the launch traced here: 38.4 us
  Pallas kernels  35 us (90%)
  local copies, waits for them, and re-layouts  2.79 us (7%)
  between operations  0.64 us (2%)
    pallas_call x1, Pallas kernels, fused_call(): pl.pallas_call(functools.partial(fused, count, depth), out_shape=(row, ro...  35 us
    unnamed x2, local copies, waits for them, and re-layouts  2.79 us

profile of v2, /device:TPU:0, one launch (start us, length us, event | category | flops | bytes accessed | tf_op | source)
XLA Modules:
  0.0 38.4 jit_solution(16743860066485345562)
XLA Ops:
  0.6 35.0 %shard_map.113 = (bf16[2,8192]{1,0:T(2,128)(2,1)}, bf16[2,8192]{1,0:T(2,128)(2,1)}) custom-call(bf16[2,8192]{1,0:T(2,128)(2,1)} %q_hbm.1, bf16[2,512,2,1024]{3,2,1,0:T(2,128)(2,1)} %cache_ref.1, s32[2]{0:T(128)} %live_hbm.1, bf16[2,8192]{1,0:T(2,128)(2,1)} %residual_hbm.1, s32[2]{0:T(128)} %bitcast.4, s32[1,16]{1,0:T(1,128)} %bitcast.5, ...), custom_call_target="tpu_custom_call" | custom-call | tf_op jit(solution)/shard_map/pallas_call | solution.py:433
  35.6 1.4 %copy.14 = bf16[2,8192]{1,0:T(2,128)(2,1)} copy(bf16[2,8192]{1,0:T(2,128)(2,1)} %get-tuple-element.4) | data formatting | bytes 65536
  37.0 1.4 %copy.15 = bf16[2,8192]{1,0:T(2,128)(2,1)} copy(bf16[2,8192]{1,0:T(2,128)(2,1)} %get-tuple-element.5) | data formatting | bytes 65536

commit v3 on v2

--- a/solution.py
+++ b/solution.py
@@ -96,6 +96,8 @@
 
 
 CHUNKS = 4
+LAG_Y = 4
+LAG_Z = 8
 LANES = 128
 
 
@@ -142,6 +144,7 @@
     shrink_out,
     shrink_in,
     part,
+    core_out,
     core_in,
     y_out,
     y_in,
@@ -311,7 +314,7 @@
         mine,
         (((1,), (1,)), ((), ())),
         preferred_element_type=jnp.float32,
-    ).reshape(count, rank, row_count)
+    ).reshape(count, rank, row_count).astype(jnp.bfloat16)
 
     def shrink_copy(peer, source):
         return remote(
@@ -336,11 +339,11 @@
 
     for copy in small_copies[len(early) :]:
         copy.wait()
-    shrink = jnp.sum(shrink_in[...], axis=0).astype(jnp.bfloat16)
+    shrink = jnp.sum(shrink_in[...].astype(jnp.float32), axis=0).astype(jnp.bfloat16)
     owned = owners == me.astype(jnp.float32)
 
     core_copies = [
-        remote(part.at[j, 1 - my_core], core_in.at[j], core_send.at[j], core_recv.at[j], core_peer)
+        remote(core_out.at[j], core_in.at[j], core_send.at[j], core_recv.at[j], core_peer)
         for j in range(CHUNKS)
     ]
     y_copies = [
@@ -357,7 +360,7 @@
             (me + 4 * step) % count,
         )
 
-    for j in range(CHUNKS):
+    def send_to_core(j):
         delta = (
             adapter_scale
             * lax.dot_general(
@@ -369,19 +372,30 @@
         ).astype(jnp.bfloat16)
         delta = jnp.where(owned, delta.astype(jnp.float32), 0.0)
         part[j] = part[j] + delta.reshape(2, count, columns)
+        core_out[j] = part[j, 1 - my_core].astype(jnp.bfloat16)
         core_copies[j].start()
-    for j in range(CHUNKS):
+
+    def send_along_y(j):
         core_copies[j].wait_recv()
-        chip_sum = part[j, my_core] + core_in[j]
+        chip_sum = part[j, my_core] + core_in[j].astype(jnp.float32)
         y_out[j] = chip_sum.reshape(2, count // 2, columns).astype(jnp.bfloat16)
         y_copies[j].start()
-    for j in range(CHUNKS):
+
+    def send_along_z(j):
         y_copies[j].wait_recv()
         pair_sum = y_out[j, my_y].astype(jnp.float32) + y_in[j].astype(jnp.float32)
         for z in range(4):
             z_out[j, z] = pair_sum[2 * z : 2 * z + 2].astype(jnp.bfloat16)
         for step in range(1, 4):
             z_copy(j, step).start()
+
+    for step in range(CHUNKS + LAG_Z):
+        if step < CHUNKS:
+            send_to_core(step)
+        if 0 <= step - LAG_Y < CHUNKS:
+            send_along_y(step - LAG_Y)
+        if 0 <= step - LAG_Z < CHUNKS:
+            send_along_z(step - LAG_Z)
     square = jnp.zeros((2, 1), jnp.float32)
     for j in range(CHUNKS):
         here = slice(j * columns, (j + 1) * columns)
@@ -450,10 +464,11 @@
             pltpu.VMEM((count, 2, depth + LANES), bf16),
             pltpu.VMEM((2 * count, depth + LANES), f32),
             pltpu.VMEM((count, rank, depth), bf16),
-            pltpu.VMEM((count, rank, 2 * count), f32),
-            pltpu.VMEM((count, rank, 2 * count), f32),
+            pltpu.VMEM((count, rank, 2 * count), bf16),
+            pltpu.VMEM((count, rank, 2 * count), bf16),
             pltpu.VMEM((CHUNKS, 2, count, columns), f32),
-            pltpu.VMEM((CHUNKS, count, columns), f32),
+            pltpu.VMEM((CHUNKS, count, columns), bf16),
+            pltpu.VMEM((CHUNKS, count, columns), bf16),
             pltpu.VMEM((CHUNKS, 2, count // 2, columns), bf16),
             pltpu.VMEM((CHUNKS, count // 2, columns), bf16),
             pltpu.VMEM((CHUNKS, 4, 2, columns), bf16),

time: 38.7 us -> 37.6 us (0.972)
  Pallas kernels: 35 us -> 33.9 us
    pallas_call x1, Pallas kernels: 35 us -> 33.9 us  [fused_call(): pl.pallas_call(functools.partial(fused, count, depth), out_shape=(row, ro...]
where the time goes in v3:
time: 37.6 us; the launch traced here: 37.4 us
  Pallas kernels  33.9 us (90%)
  local copies, waits for them, and re-layouts  2.79 us (7%)
  between operations  0.64 us (2%)
    pallas_call x1, Pallas kernels, fused_call(): pl.pallas_call(functools.partial(fused, count, depth), out_shape=(row, ro...  33.9 us
    unnamed x2, local copies, waits for them, and re-layouts  2.79 us

profile of v3, /device:TPU:0, one launch (start us, length us, event | category | flops | bytes accessed | tf_op | source)
XLA Modules:
  0.0 37.4 jit_solution(11450757138942920897)
XLA Ops:
  0.6 33.9 %shard_map.113 = (bf16[2,8192]{1,0:T(2,128)(2,1)}, bf16[2,8192]{1,0:T(2,128)(2,1)}) custom-call(bf16[2,8192]{1,0:T(2,128)(2,1)} %q_hbm.1, bf16[2,512,2,1024]{3,2,1,0:T(2,128)(2,1)} %cache_ref.1, s32[2]{0:T(128)} %live_hbm.1, bf16[2,8192]{1,0:T(2,128)(2,1)} %residual_hbm.1, s32[2]{0:T(128)} %bitcast.4, s32[1,16]{1,0:T(1,128)} %bitcast.5, ...), custom_call_target="tpu_custom_call" | custom-call | tf_op jit(solution)/shard_map/pallas_call | solution.py:447
  34.6 1.4 %copy.14 = bf16[2,8192]{1,0:T(2,128)(2,1)} copy(bf16[2,8192]{1,0:T(2,128)(2,1)} %get-tuple-element.4) | data formatting | bytes 65536
  36.0 1.4 %copy.15 = bf16[2,8192]{1,0:T(2,128)(2,1)} copy(bf16[2,8192]{1,0:T(2,128)(2,1)} %get-tuple-element.5) | data formatting | bytes 65536
